TPU v7x, 32 devices: a whole 2x2x4 slice. The times are simulated.
32 devices in a mesh: runs: 2 (over x), fibre: 16 (over z, y, core).
Axes of the slice: x: 2, y: 2, z: 4, core: 2. Of those that a mesh axis runs over, the one named last changes fastest.
Arguments:
- records: bfloat16 [2048, 1600], P(('runs', 'fibre')), parts along dimension 0, may hold values from -6 to 6
- filter_taps: bfloat16 [9, 63], replicated, may hold values from -0.25 to 0.25
- segment_ids: int32 [2048], P('runs'), parts along dimension 0, may hold values from 0 to 7, never falling along the last dimension, each value on 1 to 256 neighbouring positions
Outputs:
- correlations: bfloat16 [2048, 5, 2048], P(('runs', 'fibre')), parts along dimension 0
- source_gathers: bfloat16 [2048, 512], P(('runs', 'fibre')), parts along dimension 0
There are 2 independent parts, one for each index of `runs`. A program takes and returns all parts, laid end to end along the dimension named above; an argument that names none is the same for every part. Nothing has to cross between parts.
Inputs may be any that keep to these rules, and one draw needn't show every extreme that they name: `segment_ids`: segment numbers never fall along the fibre; each segment has 1 to 256 channels and one has exactly 256.
All inputs are finite; a program needn't handle non-finite values.
Results may differ from a plain program's by a relative error of at most 0.0073.
Values may be sent and summed in bfloat16 or wider, within the bound.
A program may use at most 128 MiB of HBM per device.

v0:
```python
import jax
import jax.numpy as jnp
from jax import lax
from jax.sharding import PartitionSpec as P

CB = 64
W = 4
F = 200
L = 400
TAPS = 63
SPAN = 9
LAGS = 32
BAND = 4


freq_parts = 4


def with_halo(block, sides, width):
    for axis, dim in sides:
        count = lax.axis_size(axis)
        forward = [(i, i + 1) for i in range(count - 1)]
        backward = [(target, source) for source, target in forward]
        low = lax.ppermute(
            lax.slice_in_dim(block, block.shape[dim] - width, None, axis=dim), axis, forward
        )
        high = lax.ppermute(lax.slice_in_dim(block, 0, width, axis=dim), axis, backward)
        block = jnp.concatenate([low, block, high], axis=dim)
    return block


def from_behind(block, axis, distance):
    devices = range(lax.axis_size(axis))
    route = [(i - distance, i) for i in devices if i - distance in devices]
    return lax.ppermute(block, axis, route)


def make_tables(filter_taps):
    extent = L + TAPS - 1
    out_time = jnp.arange(L)
    in_time = jnp.arange(extent)
    tap_index = out_time[None, :] - in_time[:, None] + (TAPS - 1)
    inside = (tap_index >= 0) & (tap_index < TAPS)
    safe_index = jnp.clip(tap_index, 0, TAPS - 1)
    toeplitz = jnp.where(inside[None], filter_taps[:, safe_index], jnp.zeros((), filter_taps.dtype))
    bin_index = jnp.arange(F)
    phase = (out_time[:, None] * bin_index[None, :] % L).astype(jnp.float32) * (2.0 * jnp.pi / L)
    window_taper = 0.5 - 0.5 * jnp.cos((out_time.astype(jnp.float32) + 0.5) * (2.0 * jnp.pi / L))
    dft_table = jnp.concatenate(
        [window_taper[:, None] * jnp.cos(phase), -window_taper[:, None] * jnp.sin(phase)], axis=1
    ).astype(jnp.bfloat16)
    lag_index = jnp.arange(LAGS) - LAGS // 2
    lag_phase = (bin_index[:, None] * lag_index[None, :] % L).astype(jnp.float32) * (
        2.0 * jnp.pi / L
    )
    scale = 1.0 / jnp.sqrt(jnp.float32(W * F))
    lag_table = (jnp.concatenate([jnp.cos(lag_phase), -jnp.sin(lag_phase)], axis=0) * scale).astype(
        jnp.bfloat16
    )
    return (toeplitz, dft_table, lag_table)


def spectra_of(padded, seg_local, toeplitz, dft_table):
    half_span = (SPAN - 1) // 2
    total = padded.shape[0]
    windows = padded.reshape(total, W, L)
    history = jnp.concatenate(
        [jnp.zeros((total, 1, TAPS - 1), padded.dtype), windows[:, :-1, L - (TAPS - 1) :]], axis=1
    )
    extended = jnp.concatenate([history, windows], axis=2)
    extent = L + TAPS - 1
    accum = jnp.zeros((CB * W, L), jnp.float32)
    for offset in range(SPAN):
        rows_in = extended[offset : offset + CB].reshape(CB * W, extent)
        product = jnp.dot(rows_in, toeplitz[offset], preferred_element_type=jnp.float32)
        keeping = (seg_local[offset : offset + CB] == seg_local[half_span : half_span + CB]).astype(
            jnp.float32
        )
        accum = accum + product * jnp.repeat(keeping, W)[:, None]
    filtered = accum.astype(jnp.bfloat16)
    spectrum = jnp.dot(filtered, dft_table, preferred_element_type=jnp.float32)
    power = jnp.mean(spectrum * spectrum, axis=-1, keepdims=True)
    return (spectrum * lax.rsqrt(power + 1e-06)).astype(jnp.bfloat16).reshape(CB, W, 2 * F)


def correlate(own, partner, lag_table):
    count = partner.shape[0]
    own_four = own.reshape(CB, W, 2, F)
    other_four = partner.reshape(count, W, 2, F)
    rotated = jnp.stack([-other_four[:, :, 1], other_four[:, :, 0]], axis=2)
    stacked = jnp.concatenate([other_four, rotated], axis=0)
    part_width = F // freq_parts
    total = jnp.zeros((CB, LAGS, count), jnp.float32)
    for portion in range(freq_parts):
        lower = portion * part_width
        cross = jnp.einsum(
            "cwrf,dwrf->fcd",
            own_four[..., lower : lower + part_width],
            stacked[..., lower : lower + part_width],
            preferred_element_type=jnp.float32,
        ).astype(jnp.bfloat16)
        parts = jnp.concatenate([cross[:, :, :count], cross[:, :, count:]], axis=0)
        table_rows = jnp.concatenate(
            [lag_table[lower : lower + part_width], lag_table[F + lower : F + lower + part_width]],
            axis=0,
        )
        total = total + jnp.einsum(
            "gcd,gl->cld", parts, table_rows, preferred_element_type=jnp.float32
        )
    return total


def pair_block(own, partner, lag_table, keeping):
    total = correlate(own, partner, lag_table)
    return (total * keeping[:, None, :]).astype(jnp.bfloat16)


def per_device(records, filter_taps, segment_ids):
    toeplitz, dft_table, lag_table = make_tables(filter_taps)
    half_span = (SPAN - 1) // 2
    device = lax.axis_index("fibre")
    padded = with_halo(records, (("fibre", 0),), half_span)
    seg_padded = jnp.concatenate(
        [
            jnp.full((half_span,), -1, jnp.int32),
            segment_ids,
            jnp.full((half_span + BAND * CB,), -1, jnp.int32),
        ]
    )
    start = device * CB
    seg_local = lax.dynamic_slice_in_dim(seg_padded, start, CB + 2 * half_span, 0)
    own = spectra_of(padded, seg_local, toeplitz, dft_table)
    own_seg = seg_local[half_span : half_span + CB]
    sources = lax.all_gather(own[:1], "fibre", axis=0, tiled=True)
    source_out = correlate(own, sources, lag_table).astype(jnp.bfloat16)
    source_out = source_out.reshape(CB, LAGS * sources.shape[0])

    def keep_for(offset):
        partner_seg = lax.dynamic_slice_in_dim(seg_padded, start + offset * CB + half_span, CB, 0)
        return (own_seg[:, None] == partner_seg[None, :]).astype(jnp.float32)

    results = [pair_block(own, own, lag_table, keep_for(0))]
    for offset in range(1, BAND + 1):
        partner = from_behind(own, "fibre", -offset)
        results.append(pair_block(own, partner, lag_table, keep_for(offset)))
    stacked_out = jnp.stack(results, axis=1).reshape(CB, BAND + 1, LAGS * CB)
    return (stacked_out, source_out)


def solution(mesh):
    return jax.shard_map(
        per_device,
        mesh=mesh,
        in_specs=(P(("runs", "fibre"), None), P(), P("runs")),
        out_specs=(P(("runs", "fibre"), None, None), P(("runs", "fibre"), None)),
        check_vma=False,
    )
```

profile of v0, /device:TPU:0, one launch (start us, length us, event | category | flops | bytes accessed | tf_op | source)
XLA Modules:
  0.0 572.2 jit_solution(2229693399547700618)
XLA Ops:
  1.4 2.4 collective-permute-start
  3.8 1.3 collective-permute-start.1
  7.5 367.4 %gather_fusion = bf16[184800,9]{1,0:T(8,128)(2,1)} fusion(bf16[9,63]{0,1:T(8,128)(2,1)S(1)} %copy.273, s32[185344]{0:T(1024)S(1)} %pad_clamp_fusion), kind=kCustom, calls=%fused_computation | custom fusion | bytes 7392000 | tf_op jit(solution)/shard_map/gather | solution.py:45
  374.9 45.4 %copy.274 = bf16[462,400,9]{0,1,2:T(8,128)(2,1)} copy(bf16[462,400,9]{2,1,0:T(8,128)(2,1)} %bitcast.235) | data formatting | bytes 6652800 | tf_op jit(solution)/shard_map/gather | solution.py:45
  420.7 4.6 select_bitcast_fusion
  425.3 2.5 multiply_convert_fusion.1
  433.1 1.3 convolution_multiply_fusion.4
  434.4 1.3 convolution_multiply_fusion.5
  435.7 1.3 convolution_multiply_fusion.6
  437.0 1.3 convolution_multiply_fusion.1
  438.3 1.3 convolution_multiply_fusion.2
  439.6 1.3 convolution_multiply_fusion.3
  441.0 1.3 convolution_multiply_fusion
  442.3 1.3 fusion.136
  443.6 1.7 multiply_reduce_fusion
  445.7 25.2 %all-gather.1 = bf16[16,4,400]{2,1,0:T(4,128)(2,1)S(1)} all-gather(bf16[1,4,400]{2,1,0:T(4,128)(2,1)S(1)} %copy.320), channel_id=2, replica_groups=mesh['runs'=2,'fibre'=16] {'fibre'}, dimensions={0}, use_global_device_ids=true | all-gather | bytes 54400 | tf_op jit(solution)/shard_map/all_gather | solution.py:134
  472.4 1.3 collective-permute-start.5
  473.7 1.3 collective-permute-start.4
  475.0 1.3 collective-permute-start.3
  476.3 1.3 collective-permute-start.2
  477.6 1.1 copy.276
  486.1 1.2 fusion.36
  488.7 1.2 fusion.34
  491.3 1.2 fusion.32
  492.8 13.4 %fusion.119 = bf16[64,32,64]{2,1,0:T(8,128)(2,1)S(1)} fusion(f32[32,64,64]{2,0,1:T(8,128)S(1)} %fusion.32, f32[32,64,64]{2,0,1:T(8,128)S(1)} %fusion.34, f32[32,64,64]{2,0,1:T(8,128)S(1)} %fusion.36, bf16[100,32,1]{0,1,2:T(8,128)(2,1)S(1)} %get-tuple-element.113, bf16[100,64,64]{2,1,0:T(8,128)(2,1)S(1)} %pad_maximum_fusion, f32[64,64]{1,0:T(8,128)S(1)} %get-tuple-element.97), kind=kOutput, calls=%fused_computation.116 | convolution fusion | flops 26869760 | bytes 2676992 | tf_op jit(solution)/shard_map/gcd,gl->cld/dot_general | solution.py:107
  507.7 0.9 copy.315
  509.7 0.9 copy.307
  513.0 0.9 copy.299
  517.5 0.9 copy.291
  524.2 1.2 fusion.4
  526.7 1.2 fusion.2
  529.3 1.2 fusion
  531.3 1.4 fusion.131
  532.7 1.2 stack.51
  536.7 1.2 fusion.12
  539.3 1.2 fusion.10
  541.8 1.2 fusion.8
  543.8 1.4 fusion.128
  545.2 1.2 stack.49
  549.3 1.2 fusion.20
  551.9 1.4 fusion.18
  554.6 1.2 fusion.16
  556.6 1.4 fusion.125
  561.4 1.2 fusion.28
  564.0 1.2 fusion.26
  566.5 1.2 fusion.24
  568.5 1.4 fusion.122
  571.0 1.0 copy-done.19
  (234 shorter events, 58.7 us)
Async XLA Ops:
  1.4 428.9 %collective-permute-start = (bf16[4,1600]{1,0:T(4,128)(2,1)S(1)}, bf16[4,1600]{1,0:T(4,128)(2,1)S(1)}, u32[]{:S(2)}, u32[]{:S(2)}) collective-permute-start(bf16[4,1600]{1,0:T(4,128)(2,1)S(1)} %get-tuple-element.81), channel_id=1, source_target_pairs={{0,1},{1,2},{2,3},{3,4},{4,5},{5,6},{6,7},{7,8},{8,9},{9,10},{10,1... | collective-permute-start | bytes 38408 | tf_op jit(solution)/shard_map/ppermute | solution.py:24
  3.8 426.5 %collective-permute-start.1 = (bf16[4,1600]{1,0:T(4,128)(2,1)S(1)}, bf16[4,1600]{1,0:T(4,128)(2,1)S(1)}, u32[]{:S(2)}, u32[]{:S(2)}) collective-permute-start(bf16[4,1600]{1,0:T(4,128)(2,1)S(1)} %get-tuple-element.82), channel_id=1, source_target_pairs={{1,0},{2,1},{3,2},{4,3},{5,4},{6,5},{7,6},{8,7},{9,8},{10,9},{11,1... | collective-permute-start | bytes 38408 | tf_op jit(solution)/shard_map/ppermute | solution.py:27
  5.3 2.1 copy-start.20
  420.7 9.6 %copy-start.3 = (bf16[64,1600]{1,0:T(8,128)(2,1)S(1)}, bf16[64,1600]{1,0:T(8,128)(2,1)}, u32[]{:S(2)}) copy-start(bf16[64,1600]{1,0:T(8,128)(2,1)} %param.3) | copy-start | bytes 614404
  441.0 2.7 copy-start.2
  472.4 35.1 %collective-permute-start.5 = (bf16[64,4,400]{2,1,0:T(4,128)(2,1)S(1)}, bf16[64,4,400]{2,1,0:T(4,128)(2,1)S(1)}, u32[]{:S(2)}, u32[]{:S(2)}) collective-permute-start(bf16[64,4,400]{2,1,0:T(4,128)(2,1)S(1)} %reshape.269), channel_id=1, source_target_pairs={{4,0},{5,1},{6,2},{7,3},{8,4},{9,5},{10,6},{11,7},{12,8},{13,9},{1... | collective-permute-start | bytes 614408 | tf_op jit(solution)/shard_map/ppermute | solution.py:35
  473.7 35.8 %collective-permute-start.4 = (bf16[64,4,400]{2,1,0:T(4,128)(2,1)S(1)}, bf16[64,4,400]{2,1,0:T(4,128)(2,1)S(1)}, u32[]{:S(2)}, u32[]{:S(2)}) collective-permute-start(bf16[64,4,400]{2,1,0:T(4,128)(2,1)S(1)} %reshape.269), channel_id=1, source_target_pairs={{3,0},{4,1},{5,2},{6,3},{7,4},{8,5},{9,6},{10,7},{11,8},{12,9},{13... | collective-permute-start | bytes 614408 | tf_op jit(solution)/shard_map/ppermute | solution.py:35
  475.0 37.7 %collective-permute-start.3 = (bf16[64,4,400]{2,1,0:T(4,128)(2,1)S(1)}, bf16[64,4,400]{2,1,0:T(4,128)(2,1)S(1)}, u32[]{:S(2)}, u32[]{:S(2)}) collective-permute-start(bf16[64,4,400]{2,1,0:T(4,128)(2,1)S(1)} %reshape.269), channel_id=1, source_target_pairs={{2,0},{3,1},{4,2},{5,3},{6,4},{7,5},{8,6},{9,7},{10,8},{11,9},{12,... | collective-permute-start | bytes 614408 | tf_op jit(solution)/shard_map/ppermute | solution.py:35
  476.3 41.0 %collective-permute-start.2 = (bf16[64,4,400]{2,1,0:T(4,128)(2,1)S(1)}, bf16[64,4,400]{2,1,0:T(4,128)(2,1)S(1)}, u32[]{:S(2)}, u32[]{:S(2)}) collective-permute-start(bf16[64,4,400]{2,1,0:T(4,128)(2,1)S(1)} %reshape.269), channel_id=1, source_target_pairs={{1,0},{2,1},{3,2},{4,3},{5,4},{6,5},{7,6},{8,7},{9,8},{10,9},{11,1... | collective-permute-start | bytes 614408 | tf_op jit(solution)/shard_map/ppermute | solution.py:35
  530.5 0.8 copy-start.7
  536.6 1.2 copy-start.17
  539.2 1.2 copy-start.16
  543.0 0.8 copy-start.6
  543.8 2.6 copy-start.15
  547.0 0.9 copy-start.14
  549.3 1.2 copy-start.13
  551.9 1.4 copy-start.12
  555.8 0.8 copy-start.5
  556.6 1.8 copy-start.11
  559.1 0.9 copy-start.10
  561.4 1.2 copy-start.9
  563.9 1.2 copy-start.8
  567.8 0.8 copy-start.4
  568.5 1.9 copy-start.18
  569.9 1.0 copy-start.1
  569.9 1.0 copy-start
  571.0 1.1 copy-start.19
where the time goes:
time: 581 us; the launch traced here: 572 us
  local copies, waits for them, and re-layouts  450 us (77%)
  matrix products  65 us (11%)
  blocking collectives  25.2 us (4%)
  other arithmetic  20.5 us (4%)
  starting transfers between devices  8.82 us (2%)
    gather x2, local copies, waits for them, and re-layouts, make_tables(): filter_taps[:, safe_index]  413 us
    dot_general x24, matrix products, correlate(): jnp.einsum('gcd,gl->cld', parts, table_rows, preferred_element_type=jnp.f...  38 us
    all_gather x1, blocking collectives, per_device(): sources = lax.all_gather(own[:1], 'fibre', axis=0, tiled=True)  25.2 us
    dot_general x24, matrix products, correlate(): jnp.einsum('cwrf,dwrf->fcd', own_four[..., lower:lower + part_width], sta...  14.9 us
  transfers between devices with their start and end apart: 6, of which 0 were waited for; matrix products, arithmetic and copies ran while one was open for 81% of the time, Pallas kernels for 0%

commit v1 on v0

v1 whole, which is shorter than its diff:
```python
import functools

import jax
import jax.numpy as jnp
import numpy as np
from jax import lax
from jax.experimental import pallas as pl
from jax.experimental.pallas import tpu as pltpu
from jax.sharding import PartitionSpec as P

CB = 64
W = 4
F = 200
L = 400
TAPS = 63
SPAN = 9
LAGS = 32
BAND = 4

HALF = SPAN // 2
LANES = 128
PART = 256
WIDE = 2 * PART
KDIM = W * WIDE
TILE = 256
DEPTH = TILE + LANES
EDGE = 8


def tables():
    time = np.arange(L)
    bins = np.arange(F)
    phase = (time[:, None] * bins[None, :] % L) * (2.0 * np.pi / L)
    taper = 0.5 - 0.5 * np.cos((time + 0.5) * (2.0 * np.pi / L))
    slack = (L % LANES) * (W - 1)
    rows = slack + WIDE
    dft = np.zeros((rows, WIDE), np.float32)
    dft[slack : slack + L, :F] = taper[:, None] * np.cos(phase)
    dft[slack : slack + L, PART : PART + F] = -taper[:, None] * np.sin(phase)
    lag = np.arange(LAGS) - LAGS // 2
    lag_phase = (lag[:, None] * bins[None, :] % L) * (2.0 * np.pi / L)
    scale = 1.0 / np.sqrt(W * F)
    lags = np.zeros((2, LAGS, PART), np.float32)
    lags[0, :, :F] = np.cos(lag_phase) * scale
    lags[1, :, :F] = -np.sin(lag_phase) * scale
    lags = jnp.asarray(lags).astype(jnp.bfloat16).astype(jnp.float32)
    return jnp.asarray(dft).astype(jnp.bfloat16), lags


def column(row):
    across = lax.broadcasted_iota(jnp.int32, (CB, CB), 1)
    down = lax.broadcasted_iota(jnp.int32, (CB, CB), 0)
    return jnp.sum(jnp.where(across == down, row, 0.0), axis=1, keepdims=True)


def build_toeplitz(taps_ref, base, toep):
    base[...] = jnp.zeros_like(base)
    base[0:SPAN, 0:TAPS] = taps_ref[...].astype(jnp.float32)
    toep[...] = jnp.zeros_like(toep)
    for e in range(SPAN):
        rows = jnp.broadcast_to(base[e : e + 1, :], (LANES, 2 * LANES))
        near = pltpu.roll(rows, 0, 1, stride=1, stride_axis=0).astype(jnp.bfloat16)
        at = e * DEPTH
        toep[at : at + LANES, 0:LANES] = near[:, LANES:]
        toep[at + LANES : at + 2 * LANES, :] = near
        toep[at + 2 * LANES : at + 3 * LANES, LANES:] = near[:, :LANES]


def fill_segments(seg_ref, segcol):
    seg = seg_ref[...].astype(jnp.float32)
    segcol[0:EDGE] = jnp.broadcast_to(column(seg[0:1])[CB - EDGE :], (EDGE, LANES))
    segcol[EDGE : EDGE + CB] = jnp.broadcast_to(column(seg[1:2]), (CB, LANES))
    segcol[EDGE + CB :] = jnp.broadcast_to(column(seg[2:3])[:EDGE], (EDGE, LANES))


def filter_and_transform(xf, segcol, xs, toep, y, dft_ref, emit):
    blocks = xs.shape[0] // CB
    own = segcol[EDGE : EDGE + CB]
    for e in range(SPAN):
        lower = EDGE - HALF + e
        keep = segcol[lower : lower + CB] == own
        for j in range(xf.shape[1] // LANES):
            part = xf[lower : lower + CB, j * LANES : (j + 1) * LANES]
            part = jnp.where(keep, part, 0.0).astype(jnp.bfloat16)
            for b in range(blocks):
                k = j - b * (TILE // LANES)
                if 0 <= k < DEPTH // LANES:
                    at = e * DEPTH + k * LANES
                    xs[b * CB : (b + 1) * CB, at : at + LANES] = part
    out = jnp.dot(xs[...], toep[...], preferred_element_type=jnp.float32)
    out = out.astype(jnp.bfloat16)
    for b in range(blocks):
        y[:, b * TILE : (b + 1) * TILE] = out[b * CB : (b + 1) * CB]
    slack = L % LANES
    for w in range(W):
        first = w * (L - slack)
        top = slack * (W - 1 - w)
        raw = jnp.dot(
            y[:, first : first + WIDE],
            dft_ref[top : top + WIDE, :],
            preferred_element_type=jnp.float32,
        )
        power = jnp.sum(raw * raw, axis=-1, keepdims=True) * (1.0 / (2 * F))
        emit(w, raw * lax.rsqrt(power + 1e-06))


def spectra_kernel(low_ref, x_ref, high_ref, taps_ref, seg_ref, dft_ref, out_ref, base, toep, segcol, xf, xs, y):
    build_toeplitz(taps_ref, base, toep)
    fill_segments(seg_ref, segcol)
    xf[...] = jnp.zeros_like(xf)
    samples = x_ref.shape[1]
    edge = low_ref.shape[0]
    xf[0:EDGE, LANES : LANES + samples] = low_ref[edge - EDGE :].astype(jnp.float32)
    xf[EDGE : EDGE + CB, LANES : LANES + samples] = x_ref[...].astype(jnp.float32)
    xf[EDGE + CB :, LANES : LANES + samples] = high_ref[0:EDGE].astype(jnp.float32)

    def emit(w, value):
        out_ref[:, w * WIDE : (w + 1) * WIDE] = value.astype(jnp.bfloat16)

    filter_and_transform(xf, segcol, xs, toep, y, dft_ref, emit)


def rotate(own_ref, lag_ref, turned):
    def put(l, w, re, im):
        rows = slice(l * CB, (l + 1) * CB)
        turned[rows, w * WIDE : w * WIDE + PART] = re.astype(jnp.bfloat16)
        turned[rows, w * WIDE + PART : (w + 1) * WIDE] = im.astype(jnp.bfloat16)

    middle = LAGS // 2
    for w in range(W):
        re = own_ref[:, w * WIDE : w * WIDE + PART].astype(jnp.float32)
        im = own_ref[:, w * WIDE + PART : (w + 1) * WIDE].astype(jnp.float32)
        for l in range(middle + 1):
            cos, sin = lag_ref[0, l : l + 1], lag_ref[1, l : l + 1]
            a, b, c, d = re * cos, im * sin, im * cos, re * sin
            put(l, w, a + b, c - d)
            if 0 < l < middle:
                put(2 * middle - l, w, a - b, c + d)


def place(total, lags, first, keeps, corr_ref, n, src_ref):
    def at(l, lower, width):
        return total[(l - first) * CB : (l - first + 1) * CB, lower : lower + width]

    for l in range(first, first + lags, 2):
        for k in range(BAND + 1):
            pair = jnp.concatenate([at(l, k * CB, CB), at(l + 1, k * CB, CB)], axis=1)
            pair = jnp.where(keeps[k], pair, 0.0)
            corr_ref[k, :, l * CB : (l + 2) * CB] = pair.astype(jnp.bfloat16)
    lower = (BAND + 1) * CB
    gathers = jnp.concatenate([at(l, lower, n) for l in range(first, first + lags)], axis=1)
    src_ref[:, first * n : (first + lags) * n] = gathers.astype(jnp.bfloat16)


def pair_masks(seg_ref):
    seg = seg_ref[...].astype(jnp.float32)
    own = column(seg[1:2])
    keeps = []
    for k in range(BAND + 1):
        row = seg[1 + k : 2 + k]
        row = jnp.concatenate([row, row], axis=1)
        keeps.append(jnp.broadcast_to(own, (CB, 2 * CB)) == row)
    return keeps


def pairs_kernel(n, own_ref, other_ref, seg_ref, lag_ref, corr_ref, src_ref, turned):
    rotate(own_ref, lag_ref, turned)
    keeps = pair_masks(seg_ref)
    group = 8
    for first in range(0, LAGS, group):
        total = lax.dot_general(
            turned[first * CB : (first + group) * CB],
            other_ref[...],
            (((1,), (1,)), ((), ())),
            preferred_element_type=jnp.float32,
        )
        place(total, group, first, keeps, corr_ref, n, src_ref)


def per_device(records, filter_taps, segment_ids):
    n = lax.axis_size("fibre")
    me = lax.axis_index("fibre")
    samples = records.shape[1]
    dft, lags = tables()
    seg = jnp.pad(segment_ids.reshape(n, CB), ((1, BAND + 1), (0, 0)), constant_values=-1)
    seg = lax.dynamic_slice_in_dim(seg, me, BAND + 3, 0)
    up = [(i, i + 1) for i in range(n - 1)]
    low = lax.ppermute(records[CB - EDGE :], "fibre", up)
    high = lax.ppermute(records[:EDGE], "fibre", [(b, a) for a, b in up])
    blocks = -(-samples // TILE)
    vmem = pl.BlockSpec(memory_space=pltpu.VMEM)
    own = pl.pallas_call(
        spectra_kernel,
        out_shape=jax.ShapeDtypeStruct((CB, KDIM), jnp.bfloat16),
        in_specs=[vmem] * 6,
        out_specs=vmem,
        scratch_shapes=[
            pltpu.VMEM((16, 2 * LANES), jnp.float32),
            pltpu.VMEM((SPAN * DEPTH, TILE), jnp.bfloat16),
            pltpu.VMEM((CB + 2 * EDGE, LANES), jnp.float32),
            pltpu.VMEM((CB + 2 * EDGE, LANES + blocks * TILE), jnp.float32),
            pltpu.VMEM((blocks * CB, SPAN * DEPTH), jnp.bfloat16),
            pltpu.VMEM((CB, blocks * TILE), jnp.bfloat16),
        ],
        compiler_params=pltpu.CompilerParams(vmem_limit_bytes=32 << 20),
        name="spectra",
    )(low, records, high, filter_taps, seg, dft)
    parts = [own]
    for k in range(1, BAND + 1):
        parts.append(lax.ppermute(own, "fibre", [(i, i - k) for i in range(k, n)]))
    parts.append(lax.all_gather(own[:1], "fibre", axis=0, tiled=True))
    corr, src = pl.pallas_call(
        functools.partial(pairs_kernel, n),
        out_shape=(
            jax.ShapeDtypeStruct((BAND + 1, CB, LAGS * CB), jnp.bfloat16),
            jax.ShapeDtypeStruct((CB, LAGS * n), jnp.bfloat16),
        ),
        in_specs=[vmem] * 4,
        out_specs=(vmem, vmem),
        scratch_shapes=[pltpu.VMEM((LAGS * CB, KDIM), jnp.bfloat16)],
        compiler_params=pltpu.CompilerParams(vmem_limit_bytes=40 << 20),
        name="pairs",
    )(own, jnp.concatenate(parts, axis=0), seg, lags)
    return corr.transpose(1, 0, 2), src


def solution(mesh):
    return jax.shard_map(
        per_device,
        mesh=mesh,
        in_specs=(P(("runs", "fibre"), None), P(), P("runs")),
        out_specs=(P(("runs", "fibre"), None, None), P(("runs", "fibre"), None)),
        check_vma=False,
    )
```

time: 581 us -> 62.1 us (0.11); the launches traced: 572 us -> 61.6 us
  local copies, waits for them, and re-layouts: 450 us -> 4.37 us
  matrix products: 65 us -> 0 us
  other arithmetic: 20.5 us -> 0 us
  blocking collectives: 25.2 us -> 36.4 us
  Pallas kernels: 0 us -> 8.15 us
    gather x2 -> x0, local copies, waits for them, and re-layouts: 413 us -> none  [make_tables(): filter_taps[:, safe_index]]
    dot_general x57 -> x0, matrix products: 65 us -> none  [the longest x24 38 us: correlate(): jnp.einsum('gcd,gl->cld', parts, table_rows, preferred_element_type=jnp.f...]
    all_gather x1, blocking collectives: 25.2 us -> 36.4 us  [per_device(): parts.append(lax.all_gather(own[:1], 'fibre', axis=0, tiled=True))]
    concatenate x34 -> x0, other arithmetic: 11.1 us -> none  [the longest x24 7.18 us: correlate(): parts = jnp.concatenate([cross[:, :, :count], cross[:, :, count:]], axis=0)]
    slice x29 -> x1, local copies, waits for them, and re-layouts: 9.16 us -> 0.77 us  [per_device(): high = lax.ppermute(records[:EDGE], 'fibre', [(b, a) for a, b in up])]
    pallas_call x0 -> x2, Pallas kernels: none -> 8.15 us  [the longest x1 5.84 us: per_device(): pl.pallas_call(functools.partial(pairs_kernel, n), out_shape=(jax.ShapeDt...]
    dot_general x24 -> x0, local copies, waits for them, and re-layouts: 7.3 us -> none  [correlate(): jnp.einsum('cwrf,dwrf->fcd', own_four[..., lower:lower + part_width], sta...]
  transfers between devices with their start and end apart: 6 -> 6, of which waited for: 0 -> 1; matrix products, arithmetic and copies ran while one was open for 81% -> 1% of each run, Pallas kernels for 0% -> 0%
where the time goes in v1:
time: 62.1 us; the launch traced here: 61.6 us
  blocking collectives  36.4 us (59%)
  starting transfers between devices  8.81 us (14%)
  Pallas kernels  8.15 us (13%)
  local copies, waits for them, and re-layouts  4.37 us (7%)
  waiting for transfers between devices  3.15 us (5%)
  between operations  0.79 us (1%)
    all_gather x1, blocking collectives, per_device(): parts.append(lax.all_gather(own[:1], 'fibre', axis=0, tiled=True))  36.4 us
    pallas_call x1, Pallas kernels, per_device(): pl.pallas_call(functools.partial(pairs_kernel, n), out_shape=(jax.ShapeDt...  5.84 us
    ppermute x4, starting transfers between devices, per_device(): parts.append(lax.ppermute(own, 'fibre', [(i, i - k) for i in range(k, n)]))  5.17 us
    ppermute x1, waiting for transfers between devices, per_device(): high = lax.ppermute(records[:EDGE], 'fibre', [(b, a) for a, b in up])  3.14 us
    unnamed x14, local copies, waits for them, and re-layouts  2.79 us
    ppermute x1, starting transfers between devices, per_device(): low = lax.ppermute(records[CB - EDGE:], 'fibre', up)  2.35 us
    pallas_call x1, Pallas kernels, per_device(): pl.pallas_call(spectra_kernel, out_shape=jax.ShapeDtypeStruct((CB, KDIM),...  2.31 us
    ppermute x1, starting transfers between devices, per_device(): high = lax.ppermute(records[:EDGE], 'fibre', [(b, a) for a, b in up])  1.29 us
  transfers between devices with their start and end apart: 6, of which 1 were waited for; matrix products, arithmetic and copies ran while one was open for 1% of the time, Pallas kernels for 0%

profile of v1, /device:TPU:0, one launch (start us, length us, event | category | flops | bytes accessed | tf_op | source)
XLA Modules:
  0.0 61.6 jit_solution(4386276276680473226)
XLA Ops:
  0.6 0.8 %fusion = (bf16[8,1600]{1,0:T(8,128)(2,1)S(1)}, bf16[8,1600]{1,0:T(8,128)(2,1)S(1)}) fusion(bf16[64,1600]{1,0:T(8,128)(2,1)} %x_ref.1), kind=kLoop, calls=%fused_computation.8 | loop fusion | bytes 102400 | tf_op jit(solution)/shard_map/slice | solution.py:189
  1.4 2.3 %collective-permute-start = (bf16[8,1600]{1,0:T(8,128)(2,1)S(1)}, bf16[8,1600]{1,0:T(8,128)(2,1)S(1)}, u32[]{:S(2)}, u32[]{:S(2)}) collective-permute-start(bf16[8,1600]{1,0:T(8,128)(2,1)S(1)} %get-tuple-element.7), channel_id=1, source_target_pairs={{0,1},{1,2},{2,3},{3,4},{4,5},{5,6},{6,7},{7,8},{8,9},{9,10},{10,1... | collective-permute-start | bytes 76808 | tf_op jit(solution)/shard_map/ppermute | solution.py:188
  3.8 1.3 %collective-permute-start.1 = (bf16[8,1600]{1,0:T(8,128)(2,1)S(1)}, bf16[8,1600]{1,0:T(8,128)(2,1)S(1)}, u32[]{:S(2)}, u32[]{:S(2)}) collective-permute-start(bf16[8,1600]{1,0:T(8,128)(2,1)S(1)} %get-tuple-element.6), channel_id=1, source_target_pairs={{1,0},{2,1},{3,2},{4,3},{5,4},{6,5},{7,6},{8,7},{9,8},{10,9},{11,1... | collective-permute-start | bytes 76808 | tf_op jit(solution)/shard_map/ppermute | solution.py:189
  5.1 0.8 %reshape.7 = s32[16,64]{1,0:T(8,128)S(1)} reshape(s32[1024]{0:T(1024)} %param.7) | data formatting | bytes 8192 | tf_op jit(solution)/shard_map/reshape | solution.py:185
  5.8 0.0 collective-permute-done.low_ref
  5.8 3.1 %collective-permute-done.1.high_ref = bf16[8,1600]{1,0:T(8,128)(2,1)S(1)} collective-permute-done((bf16[8,1600]{1,0:T(8,128)(2,1)S(1)}, bf16[8,1600]{1,0:T(8,128)(2,1)S(1)}, u32[]{:S(2)}, u32[]{:S(2)}) %collective-permute-start.1) | collective-permute-done | bytes 25632 | tf_op jit(solution)/shard_map/ppermute | solution.py:189
  9.0 0.0 copy-start
  9.0 1.1 %copy-done = bf16[560,512]{1,0:T(8,128)(2,1)S(1)} copy-done((bf16[560,512]{1,0:T(8,128)(2,1)S(1)}, bf16[560,512]{1,0:T(8,128)(2,1)}, u32[]{:S(2)}) %copy-start) | copy-done | bytes 573464
  10.0 0.0 copy-start.1
  10.0 0.9 %copy-done.1 = bf16[64,1600]{1,0:T(8,128)(2,1)S(1)} copy-done((bf16[64,1600]{1,0:T(8,128)(2,1)S(1)}, bf16[64,1600]{1,0:T(8,128)(2,1)}, u32[]{:S(2)}) %copy-start.1) | copy-done | bytes 204824
  11.0 0.0 copy-start.3
  11.0 0.7 %copy-done.3 = bf16[9,63]{1,0:T(8,128)(2,1)S(1)} copy-done((bf16[9,63]{1,0:T(8,128)(2,1)S(1)}, bf16[9,63]{1,0:T(8,128)(2,1)}, u32[]{:S(2)}) %copy-start.3) | copy-done | bytes 1158
  11.7 2.3 %spectra.1.own_ref = bf16[64,2048]{1,0:T(8,128)(2,1)S(1)} custom-call(bf16[8,1600]{1,0:T(8,128)(2,1)S(1)} %collective-permute-done.low_ref, bf16[64,1600]{1,0:T(8,128)(2,1)S(1)} %copy-done.1, bf16[8,1600]{1,0:T(8,128)(2,1)S(1)} %collective-permute-done.1.high_ref, bf16[9,63]{1,0:T(8,128)(2,1)S(1)} %copy-done.3, s32[7,64]{1,0:T(8,128)S(1)} %pad_dynamic-slice_fusion.seg_ref, ...), custom_call_target="tpu_custom_call" | custom-call | tf_op jit(solution)/shard_map/spectra/pallas_call | solution.py:192
  14.0 0.0 copy-start.2
  14.0 1.3 %collective-permute-start.2 = (bf16[64,2048]{1,0:T(8,128)(2,1)S(1)}, bf16[64,2048]{1,0:T(8,128)(2,1)S(1)}, u32[]{:S(2)}, u32[]{:S(2)}) collective-permute-start(bf16[64,2048]{1,0:T(8,128)(2,1)S(1)} %spectra.1.own_ref), channel_id=1, source_target_pairs={{1,0},{2,1},{3,2},{4,3},{5,4},{6,5},{7,6},{8,7},{9,8},{10,9},{11,1... | collective-permute-start | bytes 786440 | tf_op jit(solution)/shard_map/ppermute | solution.py:210
  15.3 1.3 %collective-permute-start.3 = (bf16[64,2048]{1,0:T(8,128)(2,1)S(1)}, bf16[64,2048]{1,0:T(8,128)(2,1)S(1)}, u32[]{:S(2)}, u32[]{:S(2)}) collective-permute-start(bf16[64,2048]{1,0:T(8,128)(2,1)S(1)} %spectra.1.own_ref), channel_id=1, source_target_pairs={{2,0},{3,1},{4,2},{5,3},{6,4},{7,5},{8,6},{9,7},{10,8},{11,9},{12,... | collective-permute-start | bytes 786440 | tf_op jit(solution)/shard_map/ppermute | solution.py:210
  16.6 1.3 %collective-permute-start.4 = (bf16[64,2048]{1,0:T(8,128)(2,1)S(1)}, bf16[64,2048]{1,0:T(8,128)(2,1)S(1)}, u32[]{:S(2)}, u32[]{:S(2)}) collective-permute-start(bf16[64,2048]{1,0:T(8,128)(2,1)S(1)} %spectra.1.own_ref), channel_id=1, source_target_pairs={{3,0},{4,1},{5,2},{6,3},{7,4},{8,5},{9,6},{10,7},{11,8},{12,9},{13... | collective-permute-start | bytes 786440 | tf_op jit(solution)/shard_map/ppermute | solution.py:210
  17.9 1.3 %collective-permute-start.5 = (bf16[64,2048]{1,0:T(8,128)(2,1)S(1)}, bf16[64,2048]{1,0:T(8,128)(2,1)S(1)}, u32[]{:S(2)}, u32[]{:S(2)}) collective-permute-start(bf16[64,2048]{1,0:T(8,128)(2,1)S(1)} %spectra.1.own_ref), channel_id=1, source_target_pairs={{4,0},{5,1},{6,2},{7,3},{8,4},{9,5},{10,6},{11,7},{12,8},{13,9},{1... | collective-permute-start | bytes 786440 | tf_op jit(solution)/shard_map/ppermute | solution.py:210
  19.2 36.4 %all-gather = bf16[16,1,2048]{2,1,0:T(2,128)(2,1)S(1)} all-gather(bf16[1,1,2048]{2,1,0:T(2,128)(2,1)S(1)} %slice_bitcast_fusion), channel_id=1, replica_groups=mesh['runs'=2,'fibre'=16] {'fibre'}, dimensions={0}, use_global_device_ids=true | all-gather | bytes 69632 | tf_op jit(solution)/shard_map/all_gather | solution.py:211
  55.6 0.0 collective-permute-done.2
  55.6 0.0 collective-permute-done.3
  55.7 0.0 collective-permute-done.4
  55.7 0.0 collective-permute-done.5
  55.8 0.0 copy-done.2
  55.8 5.8 %pairs.1 = (bf16[5,64,2048]{2,1,0:T(8,128)(2,1)}, bf16[64,512]{1,0:T(8,128)(2,1)}) custom-call(bf16[64,2048]{1,0:T(8,128)(2,1)S(1)} %spectra.1.own_ref, bf16[336,2048]{1,0:T(8,128)(2,1)S(1)} %bitcast_dynamic-update-slice_fusion.other_ref, s32[7,64]{1,0:T(8,128)S(1)} %pad_dynamic-slice_fusion.seg_ref, f32[2,32,256]{2,1,0:T(8,128)S(1)} %copy-done.2), custom_call_target="tpu_custom_call" | custom-call | tf_op jit(solution)/shard_map/pairs/pallas_call | solution.py:212
  (8 shorter events, 0.2 us)
Async XLA Ops:
  1.4 4.4 %collective-permute-start = (bf16[8,1600]{1,0:T(8,128)(2,1)S(1)}, bf16[8,1600]{1,0:T(8,128)(2,1)S(1)}, u32[]{:S(2)}, u32[]{:S(2)}) collective-permute-start(bf16[8,1600]{1,0:T(8,128)(2,1)S(1)} %get-tuple-element.7), channel_id=1, source_target_pairs={{0,1},{1,2},{2,3},{3,4},{4,5},{5,6},{6,7},{7,8},{8,9},{9,10},{10,1... | collective-permute-start | bytes 76808 | tf_op jit(solution)/shard_map/ppermute | solution.py:188
  3.8 5.2 %collective-permute-start.1 = (bf16[8,1600]{1,0:T(8,128)(2,1)S(1)}, bf16[8,1600]{1,0:T(8,128)(2,1)S(1)}, u32[]{:S(2)}, u32[]{:S(2)}) collective-permute-start(bf16[8,1600]{1,0:T(8,128)(2,1)S(1)} %get-tuple-element.6), channel_id=1, source_target_pairs={{1,0},{2,1},{3,2},{4,3},{5,4},{6,5},{7,6},{8,7},{9,8},{10,9},{11,1... | collective-permute-start | bytes 76808 | tf_op jit(solution)/shard_map/ppermute | solution.py:189
  9.0 1.1 %copy-start = (bf16[560,512]{1,0:T(8,128)(2,1)S(1)}, bf16[560,512]{1,0:T(8,128)(2,1)}, u32[]{:S(2)}) copy-start(bf16[560,512]{1,0:T(8,128)(2,1)} %constant.18.dft_ref) | copy-start | bytes 1720324
  10.0 0.9 %copy-start.1 = (bf16[64,1600]{1,0:T(8,128)(2,1)S(1)}, bf16[64,1600]{1,0:T(8,128)(2,1)}, u32[]{:S(2)}) copy-start(bf16[64,1600]{1,0:T(8,128)(2,1)} %x_ref.1) | copy-start | bytes 614404
  11.0 0.7 %copy-start.3 = (bf16[9,63]{1,0:T(8,128)(2,1)S(1)}, bf16[9,63]{1,0:T(8,128)(2,1)}, u32[]{:S(2)}) copy-start(bf16[9,63]{1,0:T(8,128)(2,1)} %taps_ref.1) | copy-start | bytes 3406
  14.0 41.8 %copy-start.2 = (f32[2,32,256]{2,1,0:T(8,128)S(1)}, f32[2,32,256]{2,1,0:T(8,128)}, u32[]{:S(2)}) copy-start(f32[2,32,256]{2,1,0:T(8,128)} %constant.20.lag_ref) | copy-start | bytes 196612
  14.0 41.6 %collective-permute-start.2 = (bf16[64,2048]{1,0:T(8,128)(2,1)S(1)}, bf16[64,2048]{1,0:T(8,128)(2,1)S(1)}, u32[]{:S(2)}, u32[]{:S(2)}) collective-permute-start(bf16[64,2048]{1,0:T(8,128)(2,1)S(1)} %spectra.1.own_ref), channel_id=1, source_target_pairs={{1,0},{2,1},{3,2},{4,3},{5,4},{6,5},{7,6},{8,7},{9,8},{10,9},{11,1... | collective-permute-start | bytes 786440 | tf_op jit(solution)/shard_map/ppermute | solution.py:210
  15.3 40.3 %collective-permute-start.3 = (bf16[64,2048]{1,0:T(8,128)(2,1)S(1)}, bf16[64,2048]{1,0:T(8,128)(2,1)S(1)}, u32[]{:S(2)}, u32[]{:S(2)}) collective-permute-start(bf16[64,2048]{1,0:T(8,128)(2,1)S(1)} %spectra.1.own_ref), channel_id=1, source_target_pairs={{2,0},{3,1},{4,2},{5,3},{6,4},{7,5},{8,6},{9,7},{10,8},{11,9},{12,... | collective-permute-start | bytes 786440 | tf_op jit(solution)/shard_map/ppermute | solution.py:210
  16.6 39.1 %collective-permute-start.4 = (bf16[64,2048]{1,0:T(8,128)(2,1)S(1)}, bf16[64,2048]{1,0:T(8,128)(2,1)S(1)}, u32[]{:S(2)}, u32[]{:S(2)}) collective-permute-start(bf16[64,2048]{1,0:T(8,128)(2,1)S(1)} %spectra.1.own_ref), channel_id=1, source_target_pairs={{3,0},{4,1},{5,2},{6,3},{7,4},{8,5},{9,6},{10,7},{11,8},{12,9},{13... | collective-permute-start | bytes 786440 | tf_op jit(solution)/shard_map/ppermute | solution.py:210
  17.9 37.8 %collective-permute-start.5 = (bf16[64,2048]{1,0:T(8,128)(2,1)S(1)}, bf16[64,2048]{1,0:T(8,128)(2,1)S(1)}, u32[]{:S(2)}, u32[]{:S(2)}) collective-permute-start(bf16[64,2048]{1,0:T(8,128)(2,1)S(1)} %spectra.1.own_ref), channel_id=1, source_target_pairs={{4,0},{5,1},{6,2},{7,3},{8,4},{9,5},{10,6},{11,7},{12,8},{13,9},{1... | collective-permute-start | bytes 786440 | tf_op jit(solution)/shard_map/ppermute | solution.py:210

commit v2 on v1

--- a/solution.py
+++ b/solution.py
@@ -25,6 +25,7 @@
 TILE = 256
 DEPTH = TILE + LANES
 EDGE = 8
+MESH = pl.DeviceIdType.MESH
 
 
 def tables():
@@ -104,22 +105,6 @@
         emit(w, raw * lax.rsqrt(power + 1e-06))
 
 
-def spectra_kernel(low_ref, x_ref, high_ref, taps_ref, seg_ref, dft_ref, out_ref, base, toep, segcol, xf, xs, y):
-    build_toeplitz(taps_ref, base, toep)
-    fill_segments(seg_ref, segcol)
-    xf[...] = jnp.zeros_like(xf)
-    samples = x_ref.shape[1]
-    edge = low_ref.shape[0]
-    xf[0:EDGE, LANES : LANES + samples] = low_ref[edge - EDGE :].astype(jnp.float32)
-    xf[EDGE : EDGE + CB, LANES : LANES + samples] = x_ref[...].astype(jnp.float32)
-    xf[EDGE + CB :, LANES : LANES + samples] = high_ref[0:EDGE].astype(jnp.float32)
-
-    def emit(w, value):
-        out_ref[:, w * WIDE : (w + 1) * WIDE] = value.astype(jnp.bfloat16)
-
-    filter_and_transform(xf, segcol, xs, toep, y, dft_ref, emit)
-
-
 def rotate(own_ref, lag_ref, turned):
     def put(l, w, re, im):
         rows = slice(l * CB, (l + 1) * CB)
@@ -138,16 +123,18 @@
                 put(2 * middle - l, w, a - b, c + d)
 
 
-def place(total, lags, first, keeps, corr_ref, n, src_ref):
+def place(total, lags, first, blocks, keeps, corr_ref, n, src_ref):
     def at(l, lower, width):
         return total[(l - first) * CB : (l - first + 1) * CB, lower : lower + width]
 
     for l in range(first, first + lags, 2):
-        for k in range(BAND + 1):
-            pair = jnp.concatenate([at(l, k * CB, CB), at(l + 1, k * CB, CB)], axis=1)
+        for i, k in enumerate(blocks):
+            pair = jnp.concatenate([at(l, i * CB, CB), at(l + 1, i * CB, CB)], axis=1)
             pair = jnp.where(keeps[k], pair, 0.0)
             corr_ref[k, :, l * CB : (l + 2) * CB] = pair.astype(jnp.bfloat16)
-    lower = (BAND + 1) * CB
+    if src_ref is None:
+        return
+    lower = len(blocks) * CB
     gathers = jnp.concatenate([at(l, lower, n) for l in range(first, first + lags)], axis=1)
     src_ref[:, first * n : (first + lags) * n] = gathers.astype(jnp.bfloat16)
 
@@ -163,18 +150,151 @@
     return keeps
 
 
-def pairs_kernel(n, own_ref, other_ref, seg_ref, lag_ref, corr_ref, src_ref, turned):
-    rotate(own_ref, lag_ref, turned)
-    keeps = pair_masks(seg_ref)
+def pair_products(n, turned, partner, blocks, keeps, corr_ref, src_ref):
     group = 8
     for first in range(0, LAGS, group):
         total = lax.dot_general(
             turned[first * CB : (first + group) * CB],
-            other_ref[...],
+            partner,
             (((1,), (1,)), ((), ())),
             preferred_element_type=jnp.float32,
         )
-        place(total, group, first, keeps, corr_ref, n, src_ref)
+        place(total, group, first, blocks, keeps, corr_ref, n, src_ref)
+
+
+def kernel(
+    n, x_ref, taps_ref, seg_ref, dft_ref, lag_ref, corr_ref, src_ref,
+    base, toep, segcol, xf, xs, y, low, high, own, others, turned, row, row_tile, rows_in, rows_wide,
+    halo_send, halo_recv, block_send, block_recv, row_send, row_recv,
+):
+    me = lax.axis_index("fibre")
+    barrier = pltpu.get_barrier_semaphore()
+
+    @pl.loop(1, n)
+    def _(d):
+        pl.semaphore_signal(barrier, inc=1, device_id={"fibre": lax.rem(me + d, n)}, device_id_type=MESH)
+
+    build_toeplitz(taps_ref, base, toep)
+    fill_segments(seg_ref, segcol)
+    keeps = pair_masks(seg_ref)
+    xf[...] = jnp.zeros_like(xf)
+    samples = x_ref.shape[1]
+    xf[EDGE : EDGE + CB, LANES : LANES + samples] = x_ref[...].astype(jnp.float32)
+    halo = low.shape[0]
+    pl.semaphore_wait(barrier, n - 1)
+
+    def remote(source, target, send, recv, device):
+        return pltpu.make_async_remote_copy(
+            src_ref=source, dst_ref=target, send_sem=send, recv_sem=recv,
+            device_id={"fibre": device}, device_id_type=MESH,
+        )
+
+    has_low, has_high = me > 0, me < n - 1
+    to_low = remote(x_ref.at[0:halo], high, halo_send.at[0], halo_recv.at[0], me - 1)
+    to_high = remote(x_ref.at[CB - halo : CB], low, halo_send.at[1], halo_recv.at[1], me + 1)
+    pl.when(has_low)(to_low.start)
+    pl.when(has_high)(to_high.start)
+
+    @pl.when(has_high)
+    def _():
+        to_low.wait_recv()
+        xf[EDGE + CB :, LANES : LANES + samples] = high[0:EDGE].astype(jnp.float32)
+
+    @pl.when(has_low)
+    def _():
+        to_high.wait_recv()
+        xf[0:EDGE, LANES : LANES + samples] = low[halo - EDGE :].astype(jnp.float32)
+
+    def emit(w, value):
+        own[:, w * WIDE : (w + 1) * WIDE] = value.astype(jnp.bfloat16)
+        for j in range(WIDE // LANES):
+            at = w * (WIDE // LANES) + j
+            row[at : at + 1, :] = value[0:1, j * LANES : (j + 1) * LANES]
+
+    filter_and_transform(xf, segcol, xs, toep, y, dft_ref, emit)
+
+    def slot(k):
+        return others.at[(k - 1) * CB : k * CB]
+
+    def block_copy(source, k, sem, device):
+        return remote(source, slot(k), block_send.at[sem], block_recv.at[k - 1], device)
+
+    even = lax.rem(me, 2) == 0
+    odd = lax.rem(me, 2) == 1
+    to_two = block_copy(own, 2, 0, me - 2)
+    to_four = block_copy(own, 4, 1, me - 4)
+    own_down = block_copy(own, 1, 2, me - 1)
+    two_down = block_copy(slot(2), 3, 3, me - 1)
+    two_up = block_copy(slot(2), 1, 2, me + 1)
+    four_up = block_copy(slot(4), 3, 3, me + 1)
+    pl.when(me >= 2)(to_two.start)
+    pl.when(me >= 4)(to_four.start)
+    pl.when(odd)(own_down.start)
+    row_tile[...] = row[...].astype(jnp.bfloat16)
+    rows_in[me] = row_tile[...]
+
+    def row_copy(d, at):
+        return remote(row_tile, rows_in.at[at], row_send.at[d], row_recv.at[at], lax.rem(me + d, n))
+
+    @pl.loop(1, n)
+    def _(d):
+        row_copy(d, me).start()
+
+    for k in range(1, BAND + 1):
+
+        @pl.when(me + k >= n)
+        def _():
+            others[(k - 1) * CB : k * CB] = jnp.zeros((CB, KDIM), jnp.bfloat16)
+
+    rotate(own, lag_ref, turned)
+
+    @pl.when(me + 2 < n)
+    def _():
+        to_two.wait_recv()
+        pl.when(even)(two_up.start)
+        pl.when(odd)(two_down.start)
+
+    pair_products(n, turned, own[...], (0,), keeps, corr_ref, None)
+
+    @pl.when(me + 4 < n)
+    def _():
+        to_four.wait_recv()
+        pl.when(even)(four_up.start)
+
+    @pl.when(me + 1 < n)
+    def _():
+        own_down.wait_recv()
+
+    pair_products(n, turned, others[0 : 2 * CB], (1, 2), keeps, corr_ref, None)
+
+    @pl.loop(1, n)
+    def _(d):
+        row_copy(d, lax.rem(me + d, n)).wait()
+
+    rows_wide[...] = rows_in[...].astype(jnp.float32)
+    for j in range(KDIM // LANES):
+        others[BAND * CB :, j * LANES : (j + 1) * LANES] = rows_wide[:, j, :].astype(jnp.bfloat16)
+
+    @pl.when(me + 3 < n)
+    def _():
+        two_down.wait_recv()
+
+    pair_products(n, turned, others[2 * CB :], (3, 4), keeps, corr_ref, src_ref)
+
+    pl.when(has_low)(to_low.wait_send)
+    pl.when(has_high)(to_high.wait_send)
+    pl.when(me >= 2)(to_two.wait_send)
+    pl.when(me >= 4)(to_four.wait_send)
+    pl.when(odd)(own_down.wait_send)
+
+    @pl.when(me + 2 < n)
+    def _():
+        pl.when(odd)(two_down.wait_send)
+        pl.when(even)(two_up.wait_send)
+
+    @pl.when(me + 4 < n)
+    def _():
+        pl.when(even)(four_up.wait_send)
 
 
 def per_device(records, filter_taps, segment_ids):
@@ -184,16 +304,18 @@
     dft, lags = tables()
     seg = jnp.pad(segment_ids.reshape(n, CB), ((1, BAND + 1), (0, 0)), constant_values=-1)
     seg = lax.dynamic_slice_in_dim(seg, me, BAND + 3, 0)
-    up = [(i, i + 1) for i in range(n - 1)]
-    low = lax.ppermute(records[CB - EDGE :], "fibre", up)
-    high = lax.ppermute(records[:EDGE], "fibre", [(b, a) for a, b in up])
     blocks = -(-samples // TILE)
     vmem = pl.BlockSpec(memory_space=pltpu.VMEM)
-    own = pl.pallas_call(
-        spectra_kernel,
-        out_shape=jax.ShapeDtypeStruct((CB, KDIM), jnp.bfloat16),
-        in_specs=[vmem] * 6,
-        out_specs=vmem,
+    dma = pltpu.SemaphoreType.DMA
+    tiles = KDIM // LANES
+    corr, src = pl.pallas_call(
+        functools.partial(kernel, n),
+        out_shape=(
+            jax.ShapeDtypeStruct((BAND + 1, CB, LAGS * CB), jnp.bfloat16),
+            jax.ShapeDtypeStruct((CB, LAGS * n), jnp.bfloat16),
+        ),
+        in_specs=[vmem] * 5,
+        out_specs=(vmem, vmem),
         scratch_shapes=[
             pltpu.VMEM((16, 2 * LANES), jnp.float32),
             pltpu.VMEM((SPAN * DEPTH, TILE), jnp.bfloat16),
@@ -201,26 +323,27 @@
             pltpu.VMEM((CB + 2 * EDGE, LANES + blocks * TILE), jnp.float32),
             pltpu.VMEM((blocks * CB, SPAN * DEPTH), jnp.bfloat16),
             pltpu.VMEM((CB, blocks * TILE), jnp.bfloat16),
+            pltpu.VMEM((2 * EDGE, samples), jnp.bfloat16),
+            pltpu.VMEM((2 * EDGE, samples), jnp.bfloat16),
+            pltpu.VMEM((CB, KDIM), jnp.bfloat16),
+            pltpu.VMEM((BAND * CB + n, KDIM), jnp.bfloat16),
+            pltpu.VMEM((LAGS * CB, KDIM), jnp.bfloat16),
+            pltpu.VMEM((tiles, LANES), jnp.float32),
+            pltpu.VMEM((tiles, LANES), jnp.bfloat16),
+            pltpu.VMEM((n, tiles, LANES), jnp.bfloat16),
+            pltpu.VMEM((n, tiles, LANES), jnp.float32),
+            dma((2,)),
+            dma((2,)),
+            dma((4,)),
+            dma((BAND,)),
+            dma((n,)),
+            dma((n,)),
         ],
-        compiler_params=pltpu.CompilerParams(vmem_limit_bytes=32 << 20),
-        name="spectra",
-    )(low, records, high, filter_taps, seg, dft)
-    parts = [own]
-    for k in range(1, BAND + 1):
-        parts.append(lax.ppermute(own, "fibre", [(i, i - k) for i in range(k, n)]))
-    parts.append(lax.all_gather(own[:1], "fibre", axis=0, tiled=True))
-    corr, src = pl.pallas_call(
-        functools.partial(pairs_kernel, n),
-        out_shape=(
-            jax.ShapeDtypeStruct((BAND + 1, CB, LAGS * CB), jnp.bfloat16),
-            jax.ShapeDtypeStruct((CB, LAGS * n), jnp.bfloat16),
+        compiler_params=pltpu.CompilerParams(
+            vmem_limit_bytes=48 << 20, collective_id=0, has_side_effects=True
         ),
-        in_specs=[vmem] * 4,
-        out_specs=(vmem, vmem),
-        scratch_shapes=[pltpu.VMEM((LAGS * CB, KDIM), jnp.bfloat16)],
-        compiler_params=pltpu.CompilerParams(vmem_limit_bytes=40 << 20),
-        name="pairs",
-    )(own, jnp.concatenate(parts, axis=0), seg, lags)
+        name="correlations",
+    )(records, filter_taps, seg, dft, lags)
     return corr.transpose(1, 0, 2), src
 
 

time: 62.1 us -> 37.3 us (0.60)
  blocking collectives: 36.4 us -> 0 us
  Pallas kernels: 8.15 us -> 30.3 us
  starting transfers between devices: 8.81 us -> 0 us
  waiting for transfers between devices: 3.15 us -> 0 us
  local copies, waits for them, and re-layouts: 4.37 us -> 5.97 us
    all_gather x1 -> x0, blocking collectives: 36.4 us -> none  [per_device(): parts.append(lax.all_gather(own[:1], 'fibre', axis=0, tiled=True))]
    pallas_call x2 -> x1, Pallas kernels: 8.15 us -> 30.3 us  [per_device(): pl.pallas_call(functools.partial(kernel, n), out_shape=(jax.ShapeDtypeStr...]
    ppermute x6 -> x0, starting transfers between devices: 8.81 us -> none  [the longest x4 5.17 us: per_device(): parts.append(lax.ppermute(own, 'fibre', [(i, i - k) for i in range(k, n)]))]
    ppermute x6 -> x0, waiting for transfers between devices: 3.15 us -> none  [the longest x1 3.14 us: per_device(): high = lax.ppermute(records[:EDGE], 'fibre', [(b, a) for a, b in up])]
    unnamed x14 -> x10, local copies, waits for them, and re-layouts: 2.79 us -> 5.2 us
    slice x1 -> x0, local copies, waits for them, and re-layouts: 0.77 us -> none  [per_device(): high = lax.ppermute(records[:EDGE], 'fibre', [(b, a) for a, b in up])]
  transfers between devices with their start and end apart: 6 -> 0, of which waited for: 1 -> 0; matrix products, arithmetic and copies ran while one was open for 1% -> 0% of each run, Pallas kernels for 0% -> 0%
where the time goes in v2:
time: 37.3 us; the launch traced here: 37 us
  Pallas kernels  30.3 us (81%)
  local copies, waits for them, and re-layouts  5.97 us (16%)
  between operations  0.66 us (2%)
    pallas_call x1, Pallas kernels, per_device(): pl.pallas_call(functools.partial(kernel, n), out_shape=(jax.ShapeDtypeStr...  30.3 us
    unnamed x10, local copies, waits for them, and re-layouts  5.2 us
    reshape x1, local copies, waits for them, and re-layouts, per_device(): segment_ids.reshape(n, CB)  0.76 us

profile of v2, /device:TPU:0, one launch (start us, length us, event | category | flops | bytes accessed | tf_op | source)
XLA Modules:
  0.0 37.0 jit_solution(5274246729238460174)
XLA Ops:
  0.6 0.8 %reshape.7 = s32[16,64]{1,0:T(8,128)S(1)} reshape(s32[1024]{0:T(1024)} %param.7) | data formatting | bytes 8192 | tf_op jit(solution)/shard_map/reshape | solution.py:305
  1.4 0.0 copy-start
  1.4 1.1 %copy-done = bf16[560,512]{1,0:T(8,128)(2,1)S(1)} copy-done((bf16[560,512]{1,0:T(8,128)(2,1)S(1)}, bf16[560,512]{1,0:T(8,128)(2,1)}, u32[]{:S(2)}) %copy-start) | copy-done | bytes 573464
  2.5 0.0 copy-start.1
  2.5 0.9 %copy-done.1 = bf16[64,1600]{1,0:T(8,128)(2,1)S(1)} copy-done((bf16[64,1600]{1,0:T(8,128)(2,1)S(1)}, bf16[64,1600]{1,0:T(8,128)(2,1)}, u32[]{:S(2)}) %copy-start.1) | copy-done | bytes 204824
  3.4 0.0 copy-start.2
  3.4 0.8 %copy-done.2 = f32[2,32,256]{2,1,0:T(8,128)S(1)} copy-done((f32[2,32,256]{2,1,0:T(8,128)S(1)}, f32[2,32,256]{2,1,0:T(8,128)}, u32[]{:S(2)}) %copy-start.2) | copy-done | bytes 65560
  4.2 0.0 copy-start.3
  4.2 0.7 %copy-done.3 = bf16[9,63]{1,0:T(8,128)(2,1)S(1)} copy-done((bf16[9,63]{1,0:T(8,128)(2,1)S(1)}, bf16[9,63]{1,0:T(8,128)(2,1)}, u32[]{:S(2)}) %copy-start.3) | copy-done | bytes 1158
  4.9 30.3 %correlations.1 = (bf16[5,64,2048]{2,1,0:T(8,128)(2,1)S(1)}, bf16[64,512]{1,0:T(8,128)(2,1)S(1)}) custom-call(bf16[64,1600]{1,0:T(8,128)(2,1)S(1)} %copy-done.1, bf16[9,63]{1,0:T(8,128)(2,1)S(1)} %copy-done.3, s32[7,64]{1,0:T(8,128)S(1)} %pad_dynamic-slice_fusion.seg_ref, bf16[560,512]{1,0:T(8,128)(2,1)S(1)} %copy-done, f32[2,32,256]{2,1,0:T(8,128)S(1)} %copy-done.2), custom_call_target="tpu_custom_call" | custom-call | tf_op jit(solution)/shard_map/correlations/pallas_call | solution.py:311
  35.3 1.1 %copy.9 = bf16[64,5,2048]{2,0,1:T(8,128)(2,1)} copy(bf16[64,5,2048]{2,0,1:T(8,128)(2,1)S(1)} %bitcast.1) | data formatting | bytes 2621440
  36.3 0.6 %copy.10 = bf16[64,512]{1,0:T(8,128)(2,1)} copy(bf16[64,512]{1,0:T(8,128)(2,1)S(1)} %get-tuple-element.9) | data formatting | bytes 131072
  (1 shorter events, 0.0 us)
Async XLA Ops:
  1.4 1.1 %copy-start = (bf16[560,512]{1,0:T(8,128)(2,1)S(1)}, bf16[560,512]{1,0:T(8,128)(2,1)}, u32[]{:S(2)}) copy-start(bf16[560,512]{1,0:T(8,128)(2,1)} %constant.18.dft_ref) | copy-start | bytes 1720324
  2.5 0.9 %copy-start.1 = (bf16[64,1600]{1,0:T(8,128)(2,1)S(1)}, bf16[64,1600]{1,0:T(8,128)(2,1)}, u32[]{:S(2)}) copy-start(bf16[64,1600]{1,0:T(8,128)(2,1)} %x_ref.1) | copy-start | bytes 614404
  3.4 0.8 %copy-start.2 = (f32[2,32,256]{2,1,0:T(8,128)S(1)}, f32[2,32,256]{2,1,0:T(8,128)}, u32[]{:S(2)}) copy-start(f32[2,32,256]{2,1,0:T(8,128)} %constant.20.lag_ref) | copy-start | bytes 196612
  4.2 0.7 %copy-start.3 = (bf16[9,63]{1,0:T(8,128)(2,1)S(1)}, bf16[9,63]{1,0:T(8,128)(2,1)}, u32[]{:S(2)}) copy-start(bf16[9,63]{1,0:T(8,128)(2,1)} %taps_ref.1) | copy-start | bytes 3406

commit v3 on v2

--- a/solution.py
+++ b/solution.py
@@ -21,7 +21,7 @@
 LANES = 128
 PART = 256
 WIDE = 2 * PART
-KDIM = W * WIDE
+PACKED = -(-2 * W * F // LANES) * LANES
 TILE = 256
 DEPTH = TILE + LANES
 EDGE = 8
@@ -41,9 +41,10 @@
     lag = np.arange(LAGS) - LAGS // 2
     lag_phase = (lag[:, None] * bins[None, :] % L) * (2.0 * np.pi / L)
     scale = 1.0 / np.sqrt(W * F)
-    lags = np.zeros((2, LAGS, PART), np.float32)
-    lags[0, :, :F] = np.cos(lag_phase) * scale
-    lags[1, :, :F] = -np.sin(lag_phase) * scale
+    cos, sin = np.cos(lag_phase) * scale, -np.sin(lag_phase) * scale
+    lags = np.zeros((2, LAGS, PACKED), np.float32)
+    lags[0, :, : 2 * W * F] = np.tile(cos, (1, 2 * W))
+    lags[1, :, : 2 * W * F] = np.tile(np.concatenate([sin, -sin], axis=1), (1, W))
     lags = jnp.asarray(lags).astype(jnp.bfloat16).astype(jnp.float32)
     return jnp.asarray(dft).astype(jnp.bfloat16), lags
 
@@ -67,14 +68,23 @@
         toep[at + 2 * LANES : at + 3 * LANES, LANES:] = near[:, :LANES]
 
 
-def fill_segments(seg_ref, segcol):
-    seg = seg_ref[...].astype(jnp.float32)
-    segcol[0:EDGE] = jnp.broadcast_to(column(seg[0:1])[CB - EDGE :], (EDGE, LANES))
-    segcol[EDGE : EDGE + CB] = jnp.broadcast_to(column(seg[1:2]), (CB, LANES))
-    segcol[EDGE + CB :] = jnp.broadcast_to(column(seg[2:3])[:EDGE], (EDGE, LANES))
-
-
-def filter_and_transform(xf, segcol, xs, toep, y, dft_ref, emit):
+def segment_row(seg_ref, block, count):
+    per_row = LANES // CB
+    at = jnp.clip(block, 0, count - 1)
+    line = seg_ref[pl.ds(at // per_row, 1), :].astype(jnp.float32)
+    row = line[:, :CB]
+    for i in range(1, per_row):
+        row = jnp.where(lax.rem(at, per_row) == i, line[:, i * CB : (i + 1) * CB], row)
+    return jnp.where((block >= 0) & (block < count), row, -1.0)
+
+
+def fill_segments(rows, segcol):
+    segcol[0:EDGE] = jnp.broadcast_to(column(rows[0])[CB - EDGE :], (EDGE, LANES))
+    segcol[EDGE : EDGE + CB] = jnp.broadcast_to(column(rows[1]), (CB, LANES))
+    segcol[EDGE + CB :] = jnp.broadcast_to(column(rows[2])[:EDGE], (EDGE, LANES))
+
+
+def filter_and_transform(xf, segcol, xs, toep, y, dft_ref):
     blocks = xs.shape[0] // CB
     own = segcol[EDGE : EDGE + CB]
     for e in range(SPAN):
@@ -93,6 +103,7 @@
     for b in range(blocks):
         y[:, b * TILE : (b + 1) * TILE] = out[b * CB : (b + 1) * CB]
     slack = L % LANES
+    packed, swapped = [], []
     for w in range(W):
         first = w * (L - slack)
         top = slack * (W - 1 - w)
@@ -102,25 +113,26 @@
             preferred_element_type=jnp.float32,
         )
         power = jnp.sum(raw * raw, axis=-1, keepdims=True) * (1.0 / (2 * F))
-        emit(w, raw * lax.rsqrt(power + 1e-06))
-
-
-def rotate(own_ref, lag_ref, turned):
-    def put(l, w, re, im):
-        rows = slice(l * CB, (l + 1) * CB)
-        turned[rows, w * WIDE : w * WIDE + PART] = re.astype(jnp.bfloat16)
-        turned[rows, w * WIDE + PART : (w + 1) * WIDE] = im.astype(jnp.bfloat16)
-
+        value = raw * lax.rsqrt(power + 1e-06)
+        re, im = value[:, :F], value[:, PART : PART + F]
+        packed += [re, im]
+        swapped += [im, re]
+    tail = [jnp.zeros((CB, PACKED - 2 * W * F), jnp.float32)]
+    return jnp.concatenate(packed + tail, axis=1), jnp.concatenate(swapped + tail, axis=1)
+
+
+def rotate(own_ref, swapped_ref, lag_ref, turned):
     middle = LAGS // 2
-    for w in range(W):
-        re = own_ref[:, w * WIDE : w * WIDE + PART].astype(jnp.float32)
-        im = own_ref[:, w * WIDE + PART : (w + 1) * WIDE].astype(jnp.float32)
+    for lower in range(0, PACKED, LANES):
+        lanes = slice(lower, lower + LANES)
+        own = own_ref[:, lanes].astype(jnp.float32)
+        swapped = swapped_ref[:, lanes].astype(jnp.float32)
         for l in range(middle + 1):
-            cos, sin = lag_ref[0, l : l + 1], lag_ref[1, l : l + 1]
-            a, b, c, d = re * cos, im * sin, im * cos, re * sin
-            put(l, w, a + b, c - d)
+            a, b = own * lag_ref[0, l : l + 1, lanes], swapped * lag_ref[1, l : l + 1, lanes]
+            turned[l * CB : (l + 1) * CB, lanes] = (a + b).astype(jnp.bfloat16)
             if 0 < l < middle:
-                put(2 * middle - l, w, a - b, c + d)
+                back = 2 * middle - l
+                turned[back * CB : (back + 1) * CB, lanes] = (a - b).astype(jnp.bfloat16)
 
 
 def place(total, lags, first, blocks, keeps, corr_ref, n, src_ref):
@@ -139,15 +151,9 @@
     src_ref[:, first * n : (first + lags) * n] = gathers.astype(jnp.bfloat16)
 
 
-def pair_masks(seg_ref):
-    seg = seg_ref[...].astype(jnp.float32)
-    own = column(seg[1:2])
-    keeps = []
-    for k in range(BAND + 1):
-        row = seg[1 + k : 2 + k]
-        row = jnp.concatenate([row, row], axis=1)
-        keeps.append(jnp.broadcast_to(own, (CB, 2 * CB)) == row)
-    return keeps
+def pair_masks(rows):
+    own = jnp.broadcast_to(column(rows[1]), (CB, 2 * CB))
+    return [own == jnp.concatenate([row, row], axis=1) for row in rows[1:]]
 
 
 def pair_products(n, turned, partner, blocks, keeps, corr_ref, src_ref):
@@ -163,11 +169,21 @@
 
 
 def kernel(
-    n, x_ref, taps_ref, seg_ref, dft_ref, lag_ref, corr_ref, src_ref,
-    base, toep, segcol, xf, xs, y, low, high, own, others, turned, row, row_tile, rows_in, rows_wide,
-    halo_send, halo_recv, block_send, block_recv, row_send, row_recv,
+    n, taps_ref, x_hbm, seg_hbm, dft_hbm, lag_hbm, corr_ref, src_ref,
+    x_ref, seg_ref, dft_ref, lag_ref,
+    base, toep, segcol, xf, xs, y, low, high, own, swapped, others, turned,
+    row, row_tile, rows_in, rows_wide,
+    load_sem, halo_send, halo_recv, block_send, block_recv, row_send, row_recv,
 ):
     me = lax.axis_index("fibre")
+    loads = [
+        pltpu.make_async_copy(source, target, load_sem.at[i])
+        for i, (source, target) in enumerate(
+            [(x_hbm, x_ref), (seg_hbm, seg_ref), (dft_hbm, dft_ref), (lag_hbm, lag_ref)]
+        )
+    ]
+    for load in loads:
+        load.start()
     barrier = pltpu.get_barrier_semaphore()
 
     @pl.loop(1, n)
@@ -175,9 +191,12 @@
         pl.semaphore_signal(barrier, inc=1, device_id={"fibre": lax.rem(me + d, n)}, device_id_type=MESH)
 
     build_toeplitz(taps_ref, base, toep)
-    fill_segments(seg_ref, segcol)
-    keeps = pair_masks(seg_ref)
     xf[...] = jnp.zeros_like(xf)
+    loads[1].wait()
+    seg_rows = [segment_row(seg_ref, me + k, n) for k in range(-1, BAND + 1)]
+    fill_segments(seg_rows, segcol)
+    keeps = pair_masks(seg_rows)
+    loads[0].wait()
     samples = x_ref.shape[1]
     xf[EDGE : EDGE + CB, LANES : LANES + samples] = x_ref[...].astype(jnp.float32)
     halo = low.shape[0]
@@ -205,13 +224,12 @@
         to_high.wait_recv()
         xf[0:EDGE, LANES : LANES + samples] = low[halo - EDGE :].astype(jnp.float32)
 
-    def emit(w, value):
-        own[:, w * WIDE : (w + 1) * WIDE] = value.astype(jnp.bfloat16)
-        for j in range(WIDE // LANES):
-            at = w * (WIDE // LANES) + j
-            row[at : at + 1, :] = value[0:1, j * LANES : (j + 1) * LANES]
-
-    filter_and_transform(xf, segcol, xs, toep, y, dft_ref, emit)
+    loads[2].wait()
+    value, turned_value = filter_and_transform(xf, segcol, xs, toep, y, dft_ref)
+    own[...] = value.astype(jnp.bfloat16)
+    swapped[...] = turned_value.astype(jnp.bfloat16)
+    for j in range(PACKED // LANES):
+        row[j : j + 1, :] = value[0:1, j * LANES : (j + 1) * LANES]
 
     def slot(k):
         return others.at[(k - 1) * CB : k * CB]
@@ -230,6 +248,7 @@
     pl.when(me >= 2)(to_two.start)
     pl.when(me >= 4)(to_four.start)
     pl.when(odd)(own_down.start)
+    row[PACKED // LANES :, :] = jnp.zeros((row.shape[0] - PACKED // LANES, LANES), jnp.float32)
     row_tile[...] = row[...].astype(jnp.bfloat16)
     rows_in[me] = row_tile[...]
 
@@ -244,9 +263,10 @@
 
         @pl.when(me + k >= n)
         def _():
-            others[(k - 1) * CB : k * CB] = jnp.zeros((CB, KDIM), jnp.bfloat16)
-
-    rotate(own, lag_ref, turned)
+            others[(k - 1) * CB : k * CB] = jnp.zeros((CB, PACKED), jnp.bfloat16)
+
+    loads[3].wait()
+    rotate(own, swapped, lag_ref, turned)
 
     @pl.when(me + 2 < n)
     def _():
@@ -272,7 +292,7 @@
         row_copy(d, lax.rem(me + d, n)).wait()
 
     rows_wide[...] = rows_in[...].astype(jnp.float32)
-    for j in range(KDIM // LANES):
+    for j in range(PACKED // LANES):
         others[BAND * CB :, j * LANES : (j + 1) * LANES] = rows_wide[:, j, :].astype(jnp.bfloat16)
 
     @pl.when(me + 3 < n)
@@ -299,24 +319,27 @@
 
 def per_device(records, filter_taps, segment_ids):
     n = lax.axis_size("fibre")
-    me = lax.axis_index("fibre")
     samples = records.shape[1]
     dft, lags = tables()
-    seg = jnp.pad(segment_ids.reshape(n, CB), ((1, BAND + 1), (0, 0)), constant_values=-1)
-    seg = lax.dynamic_slice_in_dim(seg, me, BAND + 3, 0)
+    seg = segment_ids.reshape(-1, LANES)
     blocks = -(-samples // TILE)
     vmem = pl.BlockSpec(memory_space=pltpu.VMEM)
     dma = pltpu.SemaphoreType.DMA
-    tiles = KDIM // LANES
+    hbm = pl.BlockSpec(memory_space=pltpu.HBM)
+    tiles = -(-PACKED // LANES // 16) * 16
     corr, src = pl.pallas_call(
         functools.partial(kernel, n),
         out_shape=(
             jax.ShapeDtypeStruct((BAND + 1, CB, LAGS * CB), jnp.bfloat16),
             jax.ShapeDtypeStruct((CB, LAGS * n), jnp.bfloat16),
         ),
-        in_specs=[vmem] * 5,
+        in_specs=[vmem] + [hbm] * 4,
         out_specs=(vmem, vmem),
         scratch_shapes=[
+            pltpu.VMEM(records.shape, records.dtype),
+            pltpu.VMEM(seg.shape, seg.dtype),
+            pltpu.VMEM(dft.shape, dft.dtype),
+            pltpu.VMEM(lags.shape, lags.dtype),
             pltpu.VMEM((16, 2 * LANES), jnp.float32),
             pltpu.VMEM((SPAN * DEPTH, TILE), jnp.bfloat16),
             pltpu.VMEM((CB + 2 * EDGE, LANES), jnp.float32),
@@ -325,13 +348,15 @@
             pltpu.VMEM((CB, blocks * TILE), jnp.bfloat16),
             pltpu.VMEM((2 * EDGE, samples), jnp.bfloat16),
             pltpu.VMEM((2 * EDGE, samples), jnp.bfloat16),
-            pltpu.VMEM((CB, KDIM), jnp.bfloat16),
-            pltpu.VMEM((BAND * CB + n, KDIM), jnp.bfloat16),
-            pltpu.VMEM((LAGS * CB, KDIM), jnp.bfloat16),
+            pltpu.VMEM((CB, PACKED), jnp.bfloat16),
+            pltpu.VMEM((CB, PACKED), jnp.bfloat16),
+            pltpu.VMEM((BAND * CB + n, PACKED), jnp.bfloat16),
+            pltpu.VMEM((LAGS * CB, PACKED), jnp.bfloat16),
             pltpu.VMEM((tiles, LANES), jnp.float32),
             pltpu.VMEM((tiles, LANES), jnp.bfloat16),
             pltpu.VMEM((n, tiles, LANES), jnp.bfloat16),
             pltpu.VMEM((n, tiles, LANES), jnp.float32),
+            dma((4,)),
             dma((2,)),
             dma((2,)),
             dma((4,)),
@@ -340,10 +365,10 @@
             dma((n,)),
         ],
         compiler_params=pltpu.CompilerParams(
-            vmem_limit_bytes=48 << 20, collective_id=0, has_side_effects=True
+            vmem_limit_bytes=62 << 20, collective_id=0, has_side_effects=True
         ),
         name="correlations",
-    )(records, filter_taps, seg, dft, lags)
+    )(filter_taps, records, seg, dft, lags)
     return corr.transpose(1, 0, 2), src
 
 

time: 37.3 us -> 33.3 us (0.89)
  local copies, waits for them, and re-layouts: 5.97 us -> 3.19 us
  Pallas kernels: 30.3 us -> 29.3 us
    unnamed x10 -> x4, local copies, waits for them, and re-layouts: 5.2 us -> 3.19 us
    pallas_call x1, Pallas kernels: 30.3 us -> 29.3 us  [per_device(): pl.pallas_call(functools.partial(kernel, n), out_shape=(jax.ShapeDtypeStr...]
    reshape x1 -> x0, local copies, waits for them, and re-layouts: 0.76 us -> none  [per_device(): segment_ids.reshape(n, CB)]
where the time goes in v3:
time: 33.3 us; the launch traced here: 33.1 us
  Pallas kernels  29.3 us (88%)
  local copies, waits for them, and re-layouts  3.19 us (10%)
  between operations  0.65 us (2%)
    pallas_call x1, Pallas kernels, per_device(): pl.pallas_call(functools.partial(kernel, n), out_shape=(jax.ShapeDtypeStr...  29.3 us
    unnamed x4, local copies, waits for them, and re-layouts  3.19 us

profile of v3, /device:TPU:0, one launch (start us, length us, event | category | flops | bytes accessed | tf_op | source)
XLA Modules:
  0.0 33.1 jit_solution(12989916324946296857)
XLA Ops:
  0.6 29.3 %correlations.1 = (bf16[5,64,2048]{2,1,0:T(8,128)(2,1)}, bf16[64,512]{1,0:T(8,128)(2,1)}) custom-call(bf16[9,63]{1,0:T(8,128)(2,1)} %taps_ref.1, bf16[64,1600]{1,0:T(8,128)(2,1)} %x_hbm.1, s32[8,128]{1,0:T(8,128)} %bitcast.3, bf16[560,512]{1,0:T(8,128)(2,1)} %constant.6.dft_hbm, f32[2,32,1664]{2,1,0:T(8,128)} %constant.8.lag_hbm), custom_call_target="tpu_custom_call" | custom-call | tf_op jit(solution)/shard_map/correlations/pallas_call | solution.py:330
  29.9 0.0 copy-start
  29.9 2.6 %copy.9 = bf16[64,5,2048]{2,0,1:T(8,128)(2,1)} copy(bf16[64,5,2048]{2,0,1:T(8,128)(2,1)} %bitcast.2) | data formatting | bytes 2621440
  32.5 0.0 copy-done
  32.5 0.6 %copy.10 = bf16[64,512]{1,0:T(8,128)(2,1)} copy(bf16[64,512]{1,0:T(8,128)(2,1)S(1)} %copy-done) | data formatting | bytes 131072
Async XLA Ops:
  29.9 2.6 %copy-start = (bf16[64,512]{1,0:T(8,128)(2,1)S(1)}, bf16[64,512]{1,0:T(8,128)(2,1)}, u32[]{:S(2)}) copy-start(bf16[64,512]{1,0:T(8,128)(2,1)} %get-tuple-element.9) | copy-start | bytes 196612
